TPU v7x, 32 devices: a whole 2x2x4 slice. The times are simulated.
32 devices in a mesh: req: 8 (over y, x, core), tp: 4 (over z).
Axes of the slice: x: 2, y: 2, z: 4, core: 2. Of those that a mesh axis runs over, the one named last changes fastest.
Arguments:
- queries: bfloat16 [2, 64, 2304], P(None, 'req', 'tp'), may hold values from -10 to 10
- new_keys: bfloat16 [2, 64, 2304], P(None, 'req', 'tp'), may hold values from -4 to 4
- new_values: bfloat16 [2, 64, 2304], P(None, 'req', 'tp'), may hold values from -4 to 4
- cache_keys: bfloat16 [2048, 2304], P('req', 'tp'), may hold values from -10 to 10
- cache_values: bfloat16 [2048, 2304], P('req', 'tp'), may hold values from -4 to 4
- lengths: int32 [8, 16], P('req'), may hold values from 1 to 128, 256 in all within a row
- hidden: bfloat16 [2, 64, 2304], P(None, 'req'), may hold values from -6 to 6
- gain: float32 [2304], replicated, may hold values from 0.5 to 1.5
- expert_ids: int32 [2, 64, 2], P(None, 'req'), may hold values from 0 to 7, all different within a row; in each aligned block of 8 rows (0 to 7, 8 to 15, ..., all dimensions but the last counted through in order) at most 3 rows name the same one
- route_weights: float32 [2, 64, 2], P(None, 'req'), may hold values from 0.2 to 1
- old_place: int32 [8], replicated, may hold values from 0 to 7, as said below
- new_place: int32 [8], replicated, may hold values from 0 to 7, as said below
- old_weights: bfloat16 [8, 2304, 13824], P('req', None, 'tp'), as said below
Outputs:
- context: bfloat16 [2, 64, 2304], P(None, 'req', 'tp')
- layer_out: bfloat16 [2, 64, 2304], P(None, 'req', 'tp')
- new_weights: bfloat16 [8, 2304, 13824], P('req', None, 'tp')
Inputs may be any that keep to these rules, and one draw needn't show every extreme that they name: `old_place`: every one of the 8 shards is held by at least one device; the others hold duplicates. `new_place`: every one of the 8 shards is held by at least one device; the others hold duplicates. `old_weights`: devices with equal old_place hold equal weights. `expert_ids`: in a batch, the 8 tokens of one device name one expert at most 3 times, and each token names distinct experts. `lengths`: each row sums to 256.
All inputs are finite; a program needn't handle non-finite values.
Results may differ from a plain program's by a relative error of at most 0.009.
Values may be sent and summed in bfloat16 or wider, within the bound.
No kernel may reach another device: no remote copies, remote signals or barrier semaphores. Data moves between devices by JAX's collectives and lax.ppermute only.
A program may use at most 128 MiB of HBM per device.

v0:
```python
import jax
import jax.numpy as jnp
from jax import lax
from jax.sharding import PartitionSpec as P

HEAD_SIZE = 64
EXPERTS = 8
CAP = 3


def attend(queries, new_keys, new_values, cache_keys, cache_values, lengths):
    batches, tok_rows, width = queries.shape
    heads = width // HEAD_SIZE
    pool = cache_keys.shape[0]
    scale = HEAD_SIZE ** (-0.5)
    req_lengths = lengths.reshape(-1)
    starts = jnp.cumsum(req_lengths) - req_lengths
    position = jnp.arange(pool, dtype=jnp.int32)
    owned = (position[None, :] >= starts[:, None]) & (
        position[None, :] < (starts + req_lengths)[:, None]
    )
    query_rows = queries.reshape(batches * tok_rows, heads, HEAD_SIZE)
    own_keys = new_keys.reshape(batches * tok_rows, heads, HEAD_SIZE)
    own_values = new_values.reshape(batches * tok_rows, heads, HEAD_SIZE)
    pool_keys = cache_keys.reshape(pool, heads, HEAD_SIZE)
    pool_values = cache_values.reshape(pool, heads, HEAD_SIZE)
    scores = (
        jnp.einsum("qhd,phd->hqp", query_rows, pool_keys, preferred_element_type=jnp.float32)
        * scale
    )
    scores = jnp.where(owned[None], scores, -jnp.inf)
    own_score = (
        jnp.einsum("qhd,qhd->hq", query_rows, own_keys, preferred_element_type=jnp.float32) * scale
    )
    highest = jnp.maximum(jnp.max(scores, axis=-1), own_score)
    exp_pool = jnp.exp(scores - highest[..., None])
    exp_own = jnp.exp(own_score - highest)
    denom = jnp.sum(exp_pool, axis=-1) + exp_own
    summed = jnp.einsum(
        "hqp,phd->qhd",
        exp_pool.astype(jnp.bfloat16),
        pool_values,
        preferred_element_type=jnp.float32,
    )
    prob_own = lax.optimization_barrier(exp_own.astype(jnp.bfloat16)).astype(jnp.float32)
    summed = summed + prob_own.T[:, :, None] * own_values.astype(jnp.float32)
    context = (summed / denom.T[:, :, None]).astype(jnp.bfloat16)
    return context.reshape(batches, tok_rows, width)


def choose_holders(place, me_index, nreq, shard_count):
    devices = jnp.arange(nreq, dtype=jnp.int32)
    holder = place[None, :] == jnp.arange(shard_count, dtype=jnp.int32)[:, None]
    before = (place[:, None] == place[None, :]) & (devices[:, None] < devices[None, :])
    rank_in = jnp.sum(before.astype(jnp.int32), axis=0)
    count = jnp.sum(holder.astype(jnp.int32), axis=1)
    wanted = me_index % count
    match = holder & (rank_in[None, :] == wanted[:, None])
    return jnp.sum(jnp.where(match, devices[None, :], 0), axis=1)


def expert_block(hidden_rows, chosen, weights_now, place, shard_weights, gain):
    nreq = lax.axis_size("req")
    me_index = lax.axis_index("req")
    split_count = max(1, nreq // 16)
    shard_count = EXPERTS * split_count
    tok_rows, width = hidden_rows.shape
    hid_dev = shard_weights.shape[1] // 3
    resid = hidden_rows.astype(jnp.float32)
    normed = (
        resid * gain / jnp.sqrt(jnp.mean(resid * resid, axis=-1, keepdims=True) + 1e-05)
    ).astype(jnp.bfloat16)
    flat_ids = chosen.reshape(-1)
    assigns = flat_ids.shape[0]
    shard_dest = choose_holders(place, me_index, nreq, shard_count)
    shard_list = flat_ids[:, None] * split_count + jnp.arange(split_count, dtype=jnp.int32)[None, :]
    pick = shard_list[:, :, None] == jnp.arange(shard_count, dtype=jnp.int32)[None, None, :]
    dest = jnp.sum(jnp.where(pick, shard_dest[None, None, :], 0), axis=-1)
    assign_index = jnp.arange(assigns, dtype=jnp.int32)
    earlier = (flat_ids[:, None] == flat_ids[None, :]) & (
        assign_index[None, :] < assign_index[:, None]
    )
    rank_in = jnp.sum(earlier.astype(jnp.int32), axis=1)
    slot = dest * CAP + rank_in[:, None]
    hits = jnp.any(
        slot[None, :, :] == jnp.arange(nreq * CAP, dtype=jnp.int32)[:, None, None], axis=-1
    )
    repeated = jnp.repeat(normed, assigns // tok_rows, axis=0)
    outgoing = jnp.dot(hits.astype(jnp.bfloat16), repeated, preferred_element_type=jnp.float32)
    outgoing = outgoing.astype(jnp.bfloat16).reshape(nreq, CAP, width)
    received = lax.all_to_all(outgoing, "req", split_axis=0, concat_axis=0, tiled=True)
    sources, items, feat = received.shape
    flat_rows = received.reshape(sources * items, feat)
    gate_up = jnp.dot(
        flat_rows, shard_weights[:, : 2 * hid_dev], preferred_element_type=jnp.float32
    )
    act = (jax.nn.silu(gate_up[:, :hid_dev]) * gate_up[:, hid_dev:]).astype(jnp.bfloat16)
    part = lax.dot_general(
        act,
        shard_weights[:, 2 * hid_dev :],
        (((1,), (1,)), ((), ())),
        preferred_element_type=jnp.float32,
    )
    part = part.astype(jnp.bfloat16).reshape(sources, items, feat)
    returned = lax.all_to_all(part, "req", split_axis=0, concat_axis=0, tiled=True)
    returned = returned.reshape(nreq * CAP, width)
    picked = (
        returned[slot.reshape(-1)]
        .astype(jnp.float32)
        .reshape(tok_rows, assigns // tok_rows, split_count, width)
    )
    partial_sum = jnp.einsum("rksd,rk->rd", picked, weights_now)
    tp_width = width // lax.axis_size("tp")
    tp_start = lax.axis_index("tp") * tp_width
    resid_share = lax.dynamic_slice_in_dim(resid, tp_start, tp_width, 1)
    whole = lax.psum(partial_sum.astype(jnp.bfloat16), "tp").astype(jnp.float32)
    share = lax.dynamic_slice_in_dim(whole, tp_start, tp_width, 1)
    return (resid_share + share).astype(jnp.bfloat16)


def migrate(old_weights, old_place, new_place):
    nreq = lax.axis_size("req")
    shard_count = EXPERTS * max(1, nreq // 16)
    _, width, columns = old_weights.shape
    piece = width // nreq
    pieces = old_weights.reshape(nreq, piece, columns)
    spread = lax.all_to_all(pieces, "req", split_axis=0, concat_axis=0, tiled=True)
    devices = jnp.arange(nreq, dtype=jnp.int32)
    shard_ids = jnp.arange(shard_count, dtype=jnp.int32)
    first_old = jnp.min(
        jnp.where(old_place[None, :] == shard_ids[:, None], devices[None, :], nreq), axis=1
    )
    needed = jnp.sum(
        jnp.where(new_place[:, None] == shard_ids[None, :], first_old[None, :], 0), axis=1
    )
    sending = spread[needed]
    collected = lax.all_to_all(sending, "req", split_axis=0, concat_axis=0, tiled=True)
    return collected.reshape(1, width, columns)


def on_device(
    queries,
    new_keys,
    new_values,
    cache_keys,
    cache_values,
    lengths,
    hidden,
    gain,
    expert_ids,
    route_weights,
    old_place,
    new_place,
    old_weights,
):
    context = attend(queries, new_keys, new_values, cache_keys, cache_values, lengths)
    moved = migrate(old_weights, old_place, new_place)
    first_out = expert_block(
        hidden[0], expert_ids[0], route_weights[0], old_place, old_weights[0], gain
    )
    second_out = expert_block(hidden[1], expert_ids[1], route_weights[1], new_place, moved[0], gain)
    layer_out = jnp.stack([first_out, second_out])
    return (context, layer_out, moved)


def solution(mesh):
    in_specs = (
        P(None, "req", "tp"),
        P(None, "req", "tp"),
        P(None, "req", "tp"),
        P("req", "tp"),
        P("req", "tp"),
        P("req", None),
        P(None, "req", None),
        P(),
        P(None, "req", None),
        P(None, "req", None),
        P(),
        P(),
        P("req", None, "tp"),
    )
    out_specs = (P(None, "req", "tp"), P(None, "req", "tp"), P("req", None, "tp"))
    return jax.shard_map(
        on_device, mesh=mesh, in_specs=in_specs, out_specs=out_specs, check_vma=False
    )
```

profile of v0, /device:TPU:0, one launch (start us, length us, event | category | flops | bytes accessed | tf_op | source)
XLA Modules:
  0.0 517.7 jit_solution(16262818006561352006)
XLA Ops:
  7.2 0.9 convert_reduce_fusion.2
  8.1 0.9 convert_reduce_fusion.4
  9.0 0.9 fusion.29
  10.0 0.7 fusion.60
  10.7 0.9 fusion.28
  12.2 0.9 select_reduce_fusion.5
  13.5 10.7 %all_to_all.30 = bf16[8,3,2304]{2,1,0:T(4,128)(2,1)S(1)} all-to-all(bf16[8,3,2304]{2,1,0:T(4,128)(2,1)S(1)} %reshape.523), channel_id=1, replica_groups=mesh['req'=8,'tp'=4] {'req'}, dimensions={0} | all-to-all | bytes 221184 | tf_op jit(solution)/shard_map/all_to_all | solution.py:91
  24.2 5.8 %all-to-all-start.3 = ((bf16[8,288,3456]{2,1,0:T(8,128)(2,1)}), bf16[8,288,3456]{2,1,0:T(8,128)(2,1)}, u32[]{:S(2)}, u32[]{:S(2)}) async-start(bf16[8,288,3456]{2,1,0:T(8,128)(2,1)} %bitcast.104), calls=%async_computation.3 | async-start | bytes 31850496 | tf_op jit(solution)/shard_map/all_to_all | solution.py:127
  31.0 0.7 reshape.528
  31.8 5.5 %fusion.2 = f32[24,2304]{1,0:T(8,128)S(1)} fusion(bf16[24,2304]{1,0:T(8,128)(2,1)S(1)} %reshape.524, bf16[2304,3456]{1,0:T(8,128)(2,1)} %bitcast.105), kind=kOutput, calls=%fused_computation.7 | convolution fusion | flops 254803968 | bytes 10948608 | tf_op jit(solution)/shard_map/dot_general | solution.py:94
  37.4 167.4 %all-to-all-done.3 = bf16[8,288,3456]{2,1,0:T(8,128)(2,1)} async-done(((bf16[8,288,3456]{2,1,0:T(8,128)(2,1)}), bf16[8,288,3456]{2,1,0:T(8,128)(2,1)}, u32[]{:S(2)}, u32[]{:S(2)}) %all-to-all-start.3) | async-done | bytes 15925280 | tf_op jit(solution)/shard_map/all_to_all | solution.py:127
  204.8 3.4 all-to-all-start.2
  208.1 4.1 fusion.8
  212.3 0.8 reshape.525
  213.1 6.9 %mini-gather-slice.3 = bf16[8,288,1664]{2,1,0:T(8,128)(2,1)} slice(bf16[8,288,3456]{2,1,0:T(8,128)(2,1)} %all-to-all-done.3), slice={[0:8], [0:288], [1792:3456]} | slice | bytes 15335424 | tf_op jit(solution)/shard_map/gather | solution.py:136
  220.0 7.6 %gather_fusion.3 = bf16[8,288,1664]{2,1,0:T(8,128)(2,1)} fusion(bf16[8,288,1664]{2,1,0:T(8,128)(2,1)} %mini-gather-slice.3, s32[1024]{0:T(1024)S(1)} %pad_clamp_fusion.1), kind=kCustom, calls=%fused_computation.3 | custom fusion | bytes 15335456 | tf_op jit(solution)/shard_map/gather | solution.py:136
  227.6 7.2 %mini-gather-slice.2 = bf16[8,288,1792]{2,1,0:T(8,128)(2,1)} slice(bf16[8,288,3456]{2,1,0:T(8,128)(2,1)} %all-to-all-done.3), slice={[0:8], [0:288], [0:1792]} | slice | bytes 16515072 | tf_op jit(solution)/shard_map/gather | solution.py:136
  234.8 8.0 %gather_fusion.2 = bf16[8,288,1792]{2,1,0:T(8,128)(2,1)} fusion(bf16[8,288,1792]{2,1,0:T(8,128)(2,1)} %mini-gather-slice.2, s32[1024]{0:T(1024)S(1)} %pad_clamp_fusion.1), kind=kCustom, calls=%fused_computation.2 | custom fusion | bytes 16515104 | tf_op jit(solution)/shard_map/gather | solution.py:136
  242.7 4.1 all-to-all-start.1
  246.9 13.2 %pad_maximum_fusion = bf16[8,288,3456]{2,1,0:T(8,128)(2,1)} fusion(bf16[8,288,1664]{2,1,0:T(8,128)(2,1)} %gather_fusion.3, bf16[8,288,1792]{2,1,0:T(8,128)(2,1)} %gather_fusion.2), kind=kLoop, calls=%fused_computation.4 | loop fusion | flops 31850496 | bytes 31850496
  260.1 5.8 %all-to-all-start.4 = ((bf16[8,288,3456]{2,1,0:T(8,128)(2,1)}), bf16[8,288,3456]{2,1,0:T(8,128)(2,1)}, u32[]{:S(2)}, u32[]{:S(2)}) async-start(bf16[8,288,3456]{2,1,0:T(8,128)(2,1)} %pad_maximum_fusion), calls=%async_computation.4 | async-start | bytes 31850496 | tf_op jit(solution)/shard_map/all_to_all | solution.py:137
  268.3 172.4 %all-to-all-done.4 = bf16[8,288,3456]{2,1,0:T(8,128)(2,1)} async-done(((bf16[8,288,3456]{2,1,0:T(8,128)(2,1)}), bf16[8,288,3456]{2,1,0:T(8,128)(2,1)}, u32[]{:S(2)}, u32[]{:S(2)}) %all-to-all-start.4) | async-done | bytes 15925280 | tf_op jit(solution)/shard_map/all_to_all | solution.py:137
  440.7 5.5 %fusion = f32[24,2304]{1,0:T(8,128)S(1)} fusion(bf16[24,2304]{1,0:T(8,128)(2,1)S(1)} %reshape.529, bf16[2304,3456]{1,0:T(8,128)(2,1)} %bitcast.27), kind=kOutput, calls=%fused_computation.5 | convolution fusion | flops 254803968 | bytes 10948608 | tf_op jit(solution)/shard_map/dot_general | solution.py:94
  446.2 4.2 fusion.11
  450.4 0.8 reshape.531
  451.1 3.4 all-to-all-start.5
  455.4 4.7 all-to-all-done.5
  462.1 0.7 reshape.521
  462.8 32.6 %all-reduce.3.cloned.1.call-done = (bf16[8,2304]{1,0:T(8,128)(2,1)}, bf16[8,2304]{1,0:T(8,128)(2,1)}) async-done(((bf16[8,2304]{1,0:T(8,128)(2,1)}, bf16[8,2304]{1,0:T(8,128)(2,1)}), (bf16[8,2304]{1,0:T(8,128)(2,1)}, bf16[8,2304]{1,0:T(8,128)(2,1)})) %all-reduce.3.cloned.1.call-update) | async-done | bytes 73744 | tf_op jit(solution)/shard_map/psum | solution.py:116
  495.4 0.8 fusion.40
  496.2 0.8 fusion.39
  497.6 13.3 %copy.58 = bf16[1,2304,3456]{2,1,0:T(8,128)(2,1)} copy(bf16[1,2304,3456]{2,1,0:T(8,128)(2,1)} %bitcast.34) | data formatting | bytes 31850496
  (80 shorter events, 7.9 us)
Async XLA Ops:
  7.2 259.6 %copy-start = (bf16[256,576]{0,1:T(8,128)(2,1)S(1)}, bf16[256,576]{0,1:T(8,128)(2,1)}, u32[]{:S(2)}) copy-start(bf16[256,576]{0,1:T(8,128)(2,1)} %param.16) | copy-start | bytes 884740
  24.2 6.2 %copy-start.5 = (s32[8]{0:T(128)S(1)}, s32[8]{0:T(128)}, u32[]{:S(2)}) copy-start(s32[8]{0:T(128)} %param.24) | copy-start | bytes 100
  24.2 180.6 %all-to-all-start.3 = ((bf16[8,288,3456]{2,1,0:T(8,128)(2,1)}), bf16[8,288,3456]{2,1,0:T(8,128)(2,1)}, u32[]{:S(2)}, u32[]{:S(2)}) async-start(bf16[8,288,3456]{2,1,0:T(8,128)(2,1)} %bitcast.104), calls=%async_computation.3 | async-start | bytes 31850496 | tf_op jit(solution)/shard_map/all_to_all | solution.py:127
  204.8 38.0 %all-to-all-start.2 = ((bf16[8,3,2304]{2,1,0:T(4,128)(2,1)}), bf16[8,3,2304]{2,1,0:T(4,128)(2,1)S(1)}, u32[]{:S(2)}, u32[]{:S(2)}) async-start(bf16[8,3,2304]{2,1,0:T(4,128)(2,1)} %reshape.528), calls=%async_computation.2 | async-start | bytes 294912 | tf_op jit(solution)/shard_map/all_to_all | solution.py:91
  242.7 17.3 %all-to-all-start.1 = ((bf16[8,3,2304]{2,1,0:T(4,128)(2,1)}), bf16[8,3,2304]{2,1,0:T(4,128)(2,1)S(1)}, u32[]{:S(2)}, u32[]{:S(2)}) async-start(bf16[8,3,2304]{2,1,0:T(4,128)(2,1)} %reshape.525), calls=%async_computation.1 | async-start | bytes 294912 | tf_op jit(solution)/shard_map/all_to_all | solution.py:105
  260.0 5.9 %copy-start.3 = (bf16[2,8,576]{2,1,0:T(8,128)(2,1)S(1)}, bf16[2,8,576]{2,1,0:T(8,128)(2,1)}, u32[]{:S(2)}) copy-start(bf16[2,8,576]{2,1,0:T(8,128)(2,1)} %param.13) | copy-start | bytes 55300
  260.0 6.0 %copy-start.6 = (s32[1,16]{1,0:T(1,128)S(1)}, s32[1,16]{1,0:T(1,128)}, u32[]{:S(2)}) copy-start(s32[1,16]{1,0:T(1,128)} %param.18) | copy-start | bytes 196
  260.0 6.2 %copy-start.2 = (bf16[2,8,576]{2,1,0:T(8,128)(2,1)S(1)}, bf16[2,8,576]{2,1,0:T(8,128)(2,1)}, u32[]{:S(2)}) copy-start(bf16[2,8,576]{2,1,0:T(8,128)(2,1)} %param.15) | copy-start | bytes 55300
  260.1 6.3 %copy-start.4 = (bf16[2,8,576]{2,1,0:T(8,128)(2,1)S(1)}, bf16[2,8,576]{2,1,0:T(8,128)(2,1)}, u32[]{:S(2)}) copy-start(bf16[2,8,576]{2,1,0:T(8,128)(2,1)} %param.14) | copy-start | bytes 55300
  260.1 6.9 %copy-start.7 = (f32[2,8,2]{1,2,0:T(2,128)S(1)}, f32[2,8,2]{1,2,0:T(2,128)}, u32[]{:S(2)}) copy-start(f32[2,8,2]{1,2,0:T(2,128)} %param.22) | copy-start | bytes 388
  260.1 7.4 %copy-start.1 = (bf16[2,8,2304]{2,1,0:T(8,128)(2,1)S(1)}, bf16[2,8,2304]{2,1,0:T(8,128)(2,1)}, u32[]{:S(2)}) copy-start(bf16[2,8,2304]{2,1,0:T(8,128)(2,1)} %param.19) | copy-start | bytes 221188
  260.1 180.6 %all-to-all-start.4 = ((bf16[8,288,3456]{2,1,0:T(8,128)(2,1)}), bf16[8,288,3456]{2,1,0:T(8,128)(2,1)}, u32[]{:S(2)}, u32[]{:S(2)}) async-start(bf16[8,288,3456]{2,1,0:T(8,128)(2,1)} %pad_maximum_fusion), calls=%async_computation.4 | async-start | bytes 31850496 | tf_op jit(solution)/shard_map/all_to_all | solution.py:137
  267.5 194.3 %copy-start.8 = (bf16[256,576]{0,1:T(8,128)(2,1)S(1)}, bf16[256,576]{0,1:T(8,128)(2,1)}, u32[]{:S(2)}) copy-start(bf16[256,576]{0,1:T(8,128)(2,1)} %param.17) | copy-start | bytes 884740
  451.1 9.0 %all-to-all-start.5 = ((bf16[8,3,2304]{2,1,0:T(4,128)(2,1)}), bf16[8,3,2304]{2,1,0:T(4,128)(2,1)S(1)}, u32[]{:S(2)}, u32[]{:S(2)}) async-start(bf16[8,3,2304]{2,1,0:T(4,128)(2,1)} %reshape.531), calls=%async_computation.5 | async-start | bytes 294912 | tf_op jit(solution)/shard_map/all_to_all | solution.py:105
  454.5 40.8 %all-reduce.3.cloned.1.call-start = ((), (), s32[]{:S(2)}) async-start(), calls=%async_computation.6 | async-start | bytes 147456 | tf_op jit(solution)/shard_map/psum | solution.py:116
Sparse Core Ops, SparseCore 0:
  461.9 33.4 all-reduce.2
where the time goes:
time: 519 us; the launch traced here: 518 us
  waiting for transfers between devices  377 us (73%)
  local copies, waits for them, and re-layouts  50.8 us (10%)
  starting transfers between devices  22.5 us (4%)
  other arithmetic  21.4 us (4%)
  matrix products  20.9 us (4%)
  between operations  14.4 us (3%)
  blocking collectives  10.7 us (2%)
    all_to_all x1, waiting for transfers between devices, migrate(): lax.all_to_all(sending, 'req', split_axis=0, concat_axis=0, tiled=True)  172 us
    all_to_all x1, waiting for transfers between devices, migrate(): lax.all_to_all(pieces, 'req', split_axis=0, concat_axis=0, tiled=True)  167 us
    psum x1, waiting for transfers between devices, expert_block(): whole = lax.psum(partial_sum.astype(jnp.bfloat16), 'tp').astype(jnp.float32)  32.6 us
    gather x4, local copies, waits for them, and re-layouts, migrate(): sending = spread[needed]  29.7 us
    unnamed x19, local copies, waits for them, and re-layouts  13.4 us
    unnamed x2, other arithmetic  13.3 us
    dot_general x2, matrix products, expert_block(): jnp.dot(flat_rows, shard_weights[:, :2 * hid_dev], preferred_element_type...  11.1 us
    all_to_all x1, blocking collectives, expert_block(): lax.all_to_all(outgoing, 'req', split_axis=0, concat_axis=0, tiled=True)  10.7 us
  transfers between devices with their start and end apart: 6, of which 4 were waited for; matrix products, arithmetic and copies ran while one was open for 11% of the time, Pallas kernels for 0%

commit v1 on v0

--- a/solution.py
+++ b/solution.py
@@ -59,38 +59,43 @@
     return jnp.sum(jnp.where(match, devices[None, :], 0), axis=1)
 
 
-def expert_block(hidden_rows, chosen, weights_now, place, shard_weights, gain):
+def expert_block(hidden, chosen, weights_now, place, shard_weights, gain):
     nreq = lax.axis_size("req")
     me_index = lax.axis_index("req")
     split_count = max(1, nreq // 16)
     shard_count = EXPERTS * split_count
-    tok_rows, width = hidden_rows.shape
+    batches, tok_rows, width = hidden.shape
+    topk = chosen.shape[-1]
+    tokens = batches * tok_rows
     hid_dev = shard_weights.shape[1] // 3
-    resid = hidden_rows.astype(jnp.float32)
+    resid = hidden.reshape(tokens, width).astype(jnp.float32)
     normed = (
         resid * gain / jnp.sqrt(jnp.mean(resid * resid, axis=-1, keepdims=True) + 1e-05)
     ).astype(jnp.bfloat16)
     flat_ids = chosen.reshape(-1)
     assigns = flat_ids.shape[0]
+    slots_dev = batches * CAP
     shard_dest = choose_holders(place, me_index, nreq, shard_count)
     shard_list = flat_ids[:, None] * split_count + jnp.arange(split_count, dtype=jnp.int32)[None, :]
     pick = shard_list[:, :, None] == jnp.arange(shard_count, dtype=jnp.int32)[None, None, :]
     dest = jnp.sum(jnp.where(pick, shard_dest[None, None, :], 0), axis=-1)
     assign_index = jnp.arange(assigns, dtype=jnp.int32)
-    earlier = (flat_ids[:, None] == flat_ids[None, :]) & (
-        assign_index[None, :] < assign_index[:, None]
+    batch_of = assign_index // (tok_rows * topk)
+    earlier = (
+        (flat_ids[:, None] == flat_ids[None, :])
+        & (batch_of[:, None] == batch_of[None, :])
+        & (assign_index[None, :] < assign_index[:, None])
     )
     rank_in = jnp.sum(earlier.astype(jnp.int32), axis=1)
-    slot = dest * CAP + rank_in[:, None]
-    hits = jnp.any(
-        slot[None, :, :] == jnp.arange(nreq * CAP, dtype=jnp.int32)[:, None, None], axis=-1
+    slot = dest * slots_dev + (batch_of * CAP + rank_in)[:, None]
+    slot_hit = slot[:, :, None] == jnp.arange(nreq * slots_dev, dtype=jnp.int32)[None, None, :]
+    by_token = jnp.any(slot_hit.reshape(tokens, topk * split_count, nreq * slots_dev), axis=1)
+    outgoing = jnp.dot(
+        by_token.T.astype(jnp.bfloat16), normed, preferred_element_type=jnp.float32
     )
-    repeated = jnp.repeat(normed, assigns // tok_rows, axis=0)
-    outgoing = jnp.dot(hits.astype(jnp.bfloat16), repeated, preferred_element_type=jnp.float32)
-    outgoing = outgoing.astype(jnp.bfloat16).reshape(nreq, CAP, width)
+    outgoing = outgoing.astype(jnp.bfloat16).reshape(nreq, slots_dev, width)
     received = lax.all_to_all(outgoing, "req", split_axis=0, concat_axis=0, tiled=True)
-    sources, items, feat = received.shape
-    flat_rows = received.reshape(sources * items, feat)
+    flat_rows = received.reshape(nreq * slots_dev, width)
     gate_up = jnp.dot(
         flat_rows, shard_weights[:, : 2 * hid_dev], preferred_element_type=jnp.float32
     )
@@ -101,21 +106,31 @@
         (((1,), (1,)), ((), ())),
         preferred_element_type=jnp.float32,
     )
-    part = part.astype(jnp.bfloat16).reshape(sources, items, feat)
+    part = part.astype(jnp.bfloat16).reshape(nreq, slots_dev, width)
     returned = lax.all_to_all(part, "req", split_axis=0, concat_axis=0, tiled=True)
-    returned = returned.reshape(nreq * CAP, width)
-    picked = (
-        returned[slot.reshape(-1)]
-        .astype(jnp.float32)
-        .reshape(tok_rows, assigns // tok_rows, split_count, width)
+    returned = returned.reshape(nreq * slots_dev, width)
+    coef = jnp.sum(
+        jnp.where(
+            slot_hit.reshape(tokens, topk, split_count, nreq * slots_dev),
+            weights_now.reshape(tokens, topk)[:, :, None, None],
+            0.0,
+        ),
+        axis=(1, 2),
     )
-    partial_sum = jnp.einsum("rksd,rk->rd", picked, weights_now)
+    partial_sum = jnp.dot(
+        coef,
+        returned.astype(jnp.float32),
+        precision=lax.Precision.HIGHEST,
+        preferred_element_type=jnp.float32,
+    )
     tp_width = width // lax.axis_size("tp")
     tp_start = lax.axis_index("tp") * tp_width
     resid_share = lax.dynamic_slice_in_dim(resid, tp_start, tp_width, 1)
-    whole = lax.psum(partial_sum.astype(jnp.bfloat16), "tp").astype(jnp.float32)
-    share = lax.dynamic_slice_in_dim(whole, tp_start, tp_width, 1)
-    return (resid_share + share).astype(jnp.bfloat16)
+    share = lax.psum_scatter(
+        partial_sum.astype(jnp.bfloat16), "tp", scatter_dimension=1, tiled=True
+    ).astype(jnp.float32)
+    summed = (resid_share + share).astype(jnp.bfloat16)
+    return summed.reshape(batches, tok_rows, tp_width)
 
 
 def migrate(old_weights, old_place, new_place):
@@ -155,11 +170,9 @@
 ):
     context = attend(queries, new_keys, new_values, cache_keys, cache_values, lengths)
     moved = migrate(old_weights, old_place, new_place)
-    first_out = expert_block(
-        hidden[0], expert_ids[0], route_weights[0], old_place, old_weights[0], gain
+    layer_out = expert_block(
+        hidden, expert_ids, route_weights, old_place, old_weights[0], gain
     )
-    second_out = expert_block(hidden[1], expert_ids[1], route_weights[1], new_place, moved[0], gain)
-    layer_out = jnp.stack([first_out, second_out])
     return (context, layer_out, moved)
 
 

time: 519 us -> 454 us (0.87)
  waiting for transfers between devices: 377 us -> 333 us
  matrix products: 20.9 us -> 11.9 us
  starting transfers between devices: 22.5 us -> 15 us
    psum x1 -> x0, waiting for transfers between devices: 32.6 us -> none  [expert_block(): whole = lax.psum(partial_sum.astype(jnp.bfloat16), 'tp').astype(jnp.float32)]
    all_to_all x1, waiting for transfers between devices: 172 us -> 146 us  [migrate(): lax.all_to_all(sending, 'req', split_axis=0, concat_axis=0, tiled=True)]
    unnamed x1 -> x2, waiting for transfers between devices: 0.02 us -> 22.9 us
    dot_general x2 -> x1, matrix products: 11.1 us -> 5.98 us  [expert_block(): jnp.dot(flat_rows, shard_weights[:, :2 * hid_dev], preferred_element_type...]
    unnamed x19 -> x23, local copies, waits for them, and re-layouts: 13.4 us -> 16.2 us
  transfers between devices with their start and end apart: 6 -> 4, of which waited for: 4 -> 3; matrix products, arithmetic and copies ran while one was open for 11% -> 13% of each run, Pallas kernels for 0% -> 0%
where the time goes in v1:
time: 454 us; the launch traced here: 453 us
  waiting for transfers between devices  333 us (73%)
  local copies, waits for them, and re-layouts  48.7 us (11%)
  other arithmetic  18.1 us (4%)
  starting transfers between devices  15 us (3%)
  between operations  14.3 us (3%)
  blocking collectives  12.3 us (3%)
  matrix products  11.9 us (3%)
    all_to_all x1, waiting for transfers between devices, migrate(): lax.all_to_all(pieces, 'req', split_axis=0, concat_axis=0, tiled=True)  164 us
    all_to_all x1, waiting for transfers between devices, migrate(): lax.all_to_all(sending, 'req', split_axis=0, concat_axis=0, tiled=True)  146 us
    gather x4, local copies, waits for them, and re-layouts, migrate(): sending = spread[needed]  29.7 us
    unnamed x2, waiting for transfers between devices  22.9 us
    unnamed x23, local copies, waits for them, and re-layouts  16.2 us
    unnamed x2, other arithmetic  13.3 us
    all_to_all x1, blocking collectives, expert_block(): lax.all_to_all(outgoing, 'req', split_axis=0, concat_axis=0, tiled=True)  12.3 us
  transfers between devices with their start and end apart: 4, of which 3 were waited for; matrix products, arithmetic and copies ran while one was open for 13% of the time, Pallas kernels for 0%

profile of v1, /device:TPU:0, one launch (start us, length us, event | category | flops | bytes accessed | tf_op | source)
XLA Modules:
  0.0 453.1 jit_solution(2339984218078837787)
XLA Ops:
  7.2 1.0 fusion.12
  8.3 0.9 convert_reduce_fusion.1
  9.2 0.8 copy.39
  10.1 0.1 and_select_fusion.1
  10.2 0.9 select_reduce_fusion.2
  11.1 0.2 convert_reduce_fusion
  11.7 1.2 convolution_convert_fusion
  13.0 12.3 %all_to_all.20 = bf16[8,6,2304]{2,1,0:T(8,128)(2,1)S(1)} all-to-all(bf16[8,6,2304]{2,1,0:T(8,128)(2,1)S(1)} %reshape.342), channel_id=1, replica_groups=mesh['req'=8,'tp'=4] {'req'}, dimensions={0} | all-to-all | bytes 442368 | tf_op jit(solution)/shard_map/all_to_all | solution.py:97
  25.3 5.8 %all-to-all-start.2 = ((bf16[8,288,3456]{2,1,0:T(8,128)(2,1)}), bf16[8,288,3456]{2,1,0:T(8,128)(2,1)}, u32[]{:S(2)}, u32[]{:S(2)}) async-start(bf16[8,288,3456]{2,1,0:T(8,128)(2,1)} %bitcast.50), calls=%async_computation.2 | async-start | bytes 31850496 | tf_op jit(solution)/shard_map/all_to_all | solution.py:142
  31.1 0.2 select_reduce_fusion.1
  31.3 6.0 %fusion = f32[48,2304]{1,0:T(8,128)S(1)} fusion(bf16[48,2304]{1,0:T(8,128)(2,1)S(1)} %reshape.343, bf16[2304,3456]{1,0:T(8,128)(2,1)} %bitcast.51), kind=kOutput, calls=%fused_computation.3 | convolution fusion | flops 509607936 | bytes 11280384 | tf_op jit(solution)/shard_map/dot_general | solution.py:99
  37.3 4.0 fusion.4
  41.4 0.8 reshape.344
  42.2 163.7 %all-to-all-done.2 = bf16[8,288,3456]{2,1,0:T(8,128)(2,1)} async-done(((bf16[8,288,3456]{2,1,0:T(8,128)(2,1)}), bf16[8,288,3456]{2,1,0:T(8,128)(2,1)}, u32[]{:S(2)}, u32[]{:S(2)}) %all-to-all-start.2) | async-done | bytes 15925280 | tf_op jit(solution)/shard_map/all_to_all | solution.py:142
  205.9 3.4 all-to-all-start.1
  209.3 7.2 %mini-gather-slice.2 = bf16[8,288,1792]{2,1,0:T(8,128)(2,1)} slice(bf16[8,288,3456]{2,1,0:T(8,128)(2,1)} %all-to-all-done.2), slice={[0:8], [0:288], [0:1792]} | slice | bytes 16515072 | tf_op jit(solution)/shard_map/gather | solution.py:151
  216.5 8.0 %gather_fusion = bf16[8,288,1792]{2,1,0:T(8,128)(2,1)} fusion(bf16[8,288,1792]{2,1,0:T(8,128)(2,1)} %mini-gather-slice.2, s32[1024]{0:T(1024)S(1)} %pad_clamp_fusion), kind=kCustom, calls=%fused_computation | custom fusion | bytes 16515104 | tf_op jit(solution)/shard_map/gather | solution.py:151
  224.5 6.9 %mini-gather-slice.3 = bf16[8,288,1664]{2,1,0:T(8,128)(2,1)} slice(bf16[8,288,3456]{2,1,0:T(8,128)(2,1)} %all-to-all-done.2), slice={[0:8], [0:288], [1792:3456]} | slice | bytes 15335424 | tf_op jit(solution)/shard_map/gather | solution.py:151
  231.5 7.6 %gather_fusion.1 = bf16[8,288,1664]{2,1,0:T(8,128)(2,1)} fusion(bf16[8,288,1664]{2,1,0:T(8,128)(2,1)} %mini-gather-slice.3, s32[1024]{0:T(1024)S(1)} %pad_clamp_fusion), kind=kCustom, calls=%fused_computation.1 | custom fusion | bytes 15335456 | tf_op jit(solution)/shard_map/gather | solution.py:151
  239.0 13.2 %pad_maximum_fusion = bf16[8,288,3456]{2,1,0:T(8,128)(2,1)} fusion(bf16[8,288,1664]{2,1,0:T(8,128)(2,1)} %gather_fusion.1, bf16[8,288,1792]{2,1,0:T(8,128)(2,1)} %gather_fusion), kind=kLoop, calls=%fused_computation.2 | loop fusion | flops 31850496 | bytes 31850496
  252.3 5.8 %all-to-all-start.3 = ((bf16[8,288,3456]{2,1,0:T(8,128)(2,1)}), bf16[8,288,3456]{2,1,0:T(8,128)(2,1)}, u32[]{:S(2)}, u32[]{:S(2)}) async-start(bf16[8,288,3456]{2,1,0:T(8,128)(2,1)} %pad_maximum_fusion), calls=%async_computation.3 | async-start | bytes 31850496 | tf_op jit(solution)/shard_map/all_to_all | solution.py:152
  259.0 0.2 fusion.37
  259.4 0.2 fusion.14
  259.7 0.2 convolution_convert_fusion.1
  260.0 1.1 copy.51
  261.1 0.3 fusion.10
  261.4 0.7 reshape.341
  262.1 22.8 %reduce-scatter.4.cloned.1.call-done = bf16[576,16]{1,0:T(8,128)(2,1)} async-done(((bf16[2304,16]{1,0:T(8,128)(2,1)}), bf16[576,16]{1,0:T(8,128)(2,1)}) %reduce-scatter.4.cloned.1.call-update) | async-done | bytes 18448
  284.9 1.0 copy.52
  285.9 0.7 fusion.23
  286.6 146.2 %all-to-all-done.3 = bf16[8,288,3456]{2,1,0:T(8,128)(2,1)} async-done(((bf16[8,288,3456]{2,1,0:T(8,128)(2,1)}), bf16[8,288,3456]{2,1,0:T(8,128)(2,1)}, u32[]{:S(2)}, u32[]{:S(2)}) %all-to-all-start.3) | async-done | bytes 15925280 | tf_op jit(solution)/shard_map/all_to_all | solution.py:152
  432.9 13.3 %copy.61 = bf16[1,2304,3456]{2,1,0:T(8,128)(2,1)} copy(bf16[1,2304,3456]{2,1,0:T(8,128)(2,1)} %bitcast.17) | data formatting | bytes 31850496
  (55 shorter events, 2.0 us)
Async XLA Ops:
  7.2 251.8 %copy-start = (bf16[256,576]{0,1:T(8,128)(2,1)S(1)}, bf16[256,576]{0,1:T(8,128)(2,1)}, u32[]{:S(2)}) copy-start(bf16[256,576]{0,1:T(8,128)(2,1)} %param.16) | copy-start | bytes 884740
  25.3 5.8 %copy-start.8 = (s32[8]{0:T(128)S(1)}, s32[8]{0:T(128)}, u32[]{:S(2)}) copy-start(s32[8]{0:T(128)} %param.24) | copy-start | bytes 100
  25.3 180.6 %all-to-all-start.2 = ((bf16[8,288,3456]{2,1,0:T(8,128)(2,1)}), bf16[8,288,3456]{2,1,0:T(8,128)(2,1)}, u32[]{:S(2)}, u32[]{:S(2)}) async-start(bf16[8,288,3456]{2,1,0:T(8,128)(2,1)} %bitcast.50), calls=%async_computation.2 | async-start | bytes 31850496 | tf_op jit(solution)/shard_map/all_to_all | solution.py:142
  205.9 46.4 %all-to-all-start.1 = ((bf16[8,6,2304]{2,1,0:T(8,128)(2,1)}), bf16[8,6,2304]{2,1,0:T(8,128)(2,1)S(1)}, u32[]{:S(2)}, u32[]{:S(2)}) async-start(bf16[8,6,2304]{2,1,0:T(8,128)(2,1)} %reshape.344), calls=%async_computation.1 | async-start | bytes 589824 | tf_op jit(solution)/shard_map/all_to_all | solution.py:110
  252.2 5.9 %copy-start.5 = (f32[2,8,2]{1,2,0:T(2,128)S(1)}, f32[2,8,2]{1,2,0:T(2,128)}, u32[]{:S(2)}) copy-start(f32[2,8,2]{1,2,0:T(2,128)} %param.22) | copy-start | bytes 388
  252.2 6.0 %copy-start.6 = (s32[1,16]{1,0:T(1,128)S(1)}, s32[1,16]{1,0:T(1,128)}, u32[]{:S(2)}) copy-start(s32[1,16]{1,0:T(1,128)} %param.18) | copy-start | bytes 196
  252.2 6.3 %copy-start.3 = (bf16[2,8,576]{2,1,0:T(8,128)(2,1)S(1)}, bf16[2,8,576]{2,1,0:T(8,128)(2,1)}, u32[]{:S(2)}) copy-start(bf16[2,8,576]{2,1,0:T(8,128)(2,1)} %param.13) | copy-start | bytes 55300
  252.2 6.4 %copy-start.4 = (bf16[2,8,576]{2,1,0:T(8,128)(2,1)S(1)}, bf16[2,8,576]{2,1,0:T(8,128)(2,1)}, u32[]{:S(2)}) copy-start(bf16[2,8,576]{2,1,0:T(8,128)(2,1)} %param.14) | copy-start | bytes 55300
  252.2 7.0 %copy-start.2 = (bf16[2,8,576]{2,1,0:T(8,128)(2,1)S(1)}, bf16[2,8,576]{2,1,0:T(8,128)(2,1)}, u32[]{:S(2)}) copy-start(bf16[2,8,576]{2,1,0:T(8,128)(2,1)} %param.15) | copy-start | bytes 55300
  252.2 7.4 %copy-start.1 = (bf16[2,8,2304]{2,1,0:T(8,128)(2,1)S(1)}, bf16[2,8,2304]{2,1,0:T(8,128)(2,1)}, u32[]{:S(2)}) copy-start(bf16[2,8,2304]{2,1,0:T(8,128)(2,1)} %param.19) | copy-start | bytes 221188
  252.3 8.8 %copy-start.7 = (bf16[256,576]{0,1:T(8,128)(2,1)S(1)}, bf16[256,576]{0,1:T(8,128)(2,1)}, u32[]{:S(2)}) copy-start(bf16[256,576]{0,1:T(8,128)(2,1)} %param.17) | copy-start | bytes 884740
  252.3 180.6 %all-to-all-start.3 = ((bf16[8,288,3456]{2,1,0:T(8,128)(2,1)}), bf16[8,288,3456]{2,1,0:T(8,128)(2,1)}, u32[]{:S(2)}, u32[]{:S(2)}) async-start(bf16[8,288,3456]{2,1,0:T(8,128)(2,1)} %pad_maximum_fusion), calls=%async_computation.3 | async-start | bytes 31850496 | tf_op jit(solution)/shard_map/all_to_all | solution.py:152
  258.1 26.9 %reduce-scatter.4.cloned.1.call-start = ((), (), s32[]{:S(2)}) async-start(), calls=%async_computation.5 | async-start | bytes 737280
Sparse Core Ops, SparseCore 0:
  261.2 23.6 reduce-scatter.3
